TPU v7x, 512 devices: a whole 4x4x16 slice. The times are simulated.
512 devices in a mesh: blk: 64 (over x_lo, z, core), tp: 8 (over y, x_hi).
Axes of the slice: x: 4 (x_hi: 2, x_lo: 2; x = x_hi * 2 + x_lo), y: 4, z: 16, core: 2. Of those that a mesh axis runs over, the one named last changes fastest.
Arguments:
- params: float32 [64, 4096, 1024], P('blk', None, 'tp'), may hold values from -6 to 6
- warm: float32 [64, 8, 1024], P('blk', None, 'tp'), may hold values from -6 to 6
Outputs:
- new_params: float32 [64, 4096, 1024], P('blk', None, 'tp')
- next_warm: float32 [64, 8, 1024], P('blk', None, 'tp')
All inputs are finite; a program needn't handle non-finite values.
Results may differ from a plain program's by a relative error of at most 0.0003.
Values sent between devices are 32-bit elements; how exact they have to be, the bound alone decides.
No kernel may reach another device: no remote copies, remote signals or barrier semaphores. Data moves between devices by JAX's collectives and lax.ppermute only.
A program may use at most 64 MiB of HBM per device.

v0:
```python
import jax
import jax.numpy as jnp
from jax import lax
from jax.experimental import pallas as pl
from jax.experimental.pallas import tpu as pltpu
from jax.sharding import PartitionSpec as P

GOSSIP_RATE = 0.5
TILES = 4
SIXTEENTHS = 11
RUNS = 2


def kernel_call(body, out_shape, flops, moved, **blocks):
    return pl.pallas_call(
        body,
        out_shape=out_shape,
        **blocks,
        compiler_params=pltpu.CompilerParams(vmem_limit_bytes=24 << 20),
        cost_estimate=pl.CostEstimate(flops=flops, bytes_accessed=moved, transcendentals=0),
    )


def three_parts(value):
    high = value.astype(jnp.bfloat16)
    rest = value - high.astype(jnp.float32)
    middle = rest.astype(jnp.bfloat16)
    low = (rest - middle.astype(jnp.float32)).astype(jnp.bfloat16)
    return high, middle, low


def stack(parts):
    return jnp.concatenate([p.astype(jnp.float32) for p in parts], axis=0).astype(jnp.bfloat16)


def bf16_dot(a, b, a_dim, b_dim):
    return lax.dot_general(
        a, b, (((a_dim,), (b_dim,)), ((), ())), preferred_element_type=jnp.float32
    )


def split_product(rows, parts, contract):
    rank = rows.shape[0]
    stacked = stack(three_parts(rows))
    total = None
    for taken, part in reversed(list(zip((3, 2, 1), parts))):
        products = bf16_dot(stacked[:taken * rank], part, 1, contract)
        for index in reversed(range(taken)):
            term = products[index * rank:(index + 1) * rank]
            total = term if total is None else total + term
    return total


def gram_of(rows):
    rank = rows.shape[0]
    stacked = stack(three_parts(rows))
    products = bf16_dot(stacked, stacked, 1, 1)
    total = None
    for i, j in ((1, 1), (0, 2), (2, 0), (0, 1), (1, 0), (0, 0)):
        term = products[i * rank:(i + 1) * rank, j * rank:(j + 1) * rank]
        total = term if total is None else total + term
    return total


def outer_product(values, weights):
    left, right = three_parts(values), three_parts(weights)
    pairs = ((1, 1), (0, 2), (2, 0), (0, 1), (1, 0), (0, 0))
    return bf16_dot(stack([left[i] for i, _ in pairs]), stack([right[j] for _, j in pairs]), 0, 0)


def factorize(gram, shape):
    rank = gram.shape[0]
    row_index = lax.broadcasted_iota(jnp.int32, shape, 0)
    columns = [jnp.broadcast_to(gram[:, k:k + 1], shape) for k in range(rank)]
    pivots = jnp.ones(shape, jnp.float32)
    ratios = []
    for k in range(rank):
        pivot = columns[k][k:k + 1, :]
        pivots = jnp.where(row_index == k, pivot, pivots)
        if k + 1 < rank:
            ratio = jnp.where(row_index > k, columns[k] * (1.0 / pivot), 0.0)
            ratios.append(ratio)
            for j in range(k + 1, rank):
                columns[j] = columns[j] - ratio * columns[j][k:k + 1, :]
    return pivots, ratios


def forward_substitute(ratios, value):
    for k, ratio in enumerate(ratios):
        value = value - ratio * value[k:k + 1, :]
    return value


def back_substitute(ratios, value):
    row_index = lax.broadcasted_iota(jnp.int32, value.shape, 0)
    for k in reversed(range(len(ratios))):
        below = jnp.sum(ratios[k] * value, axis=0, keepdims=True)
        value = jnp.where(row_index == k, value - below, value)
    return value


def own_product(q_hbm, matrix_hbm, packed_ref, parts_ref, main_ref, late_ref, q_vmem, sems):
    split = main_ref.shape[0]
    rows = split + late_ref.shape[0]
    pieces = [(split, rows), (0, split)]
    places = [late_ref, main_ref]
    copies = [pltpu.make_async_copy(q_hbm.at[0], q_vmem, sems.at[TILES])]
    for index, (start, end) in enumerate(pieces):
        piece = pl.ds(start, end - start)
        copies.append(pltpu.make_async_copy(matrix_hbm.at[0, piece], places[index], sems.at[index]))
    for copy in copies:
        copy.start()
    copies[0].wait()
    q = q_vmem[...]
    packed_ref[:, rows:] = q
    for index, (start, end) in enumerate(pieces):
        copies[index + 1].wait()
        parts = three_parts(places[index][...].T)
        for number, part in enumerate(parts):
            parts_ref[number, :, start:end] = part
        packed_ref[:, start:end] = split_product(q, parts, 0)


def spread_first(packed_ref, parts_ref, out_ref):
    rows = parts_ref.shape[2]
    mine = split_product(packed_ref[:, rows:], [parts_ref[i] for i in range(3)], 0)
    part = packed_ref[:, :rows] - mine
    for peer in range(out_ref.shape[0]):
        out_ref[peer] = part


def total_of(sums_ref):
    value = sums_ref[0]
    for peer in range(1, sums_ref.shape[0]):
        value = value + sums_ref[peer]
    return value


def add_up(sums_ref, out_ref):
    out_ref[...] = total_of(sums_ref)


def split_difference(mine_ref, left_ref, delta_ref, turned_ref):
    difference = left_ref[...] - mine_ref[...]
    for index, part in enumerate(three_parts(difference)):
        delta_ref[index] = part
    for index, part in enumerate(three_parts(difference.T)):
        turned_ref[index] = part


def middle_main(sum_ref, other_ref, main_ref, value_ref, image_ref, scale_ref, ratios_ref):
    split = main_ref.shape[1]
    value = sum_ref[...] + other_ref[...]
    value_ref[...] = value[:, split:]
    image_ref[...] = split_product(value[:, :split], [main_ref[i] for i in range(3)], 0)
    pivots, ratios = factorize(gram_of(value), image_ref.shape)
    scale_ref[...] = 1.0 / jnp.sqrt(pivots)
    for index, ratio in enumerate(ratios):
        ratios_ref[index] = ratio


def middle_late(value_ref, image_ref, scale_ref, ratios_ref, turned_ref, mine_ref, left_ref, late_ref, out_ref):
    split = turned_ref.shape[2]
    late = three_parts(left_ref[...] - mine_ref[...])
    for index, part in enumerate(late):
        late_ref[index] = part
    image = image_ref[...] + split_product(value_ref[...], late, 0)
    factor = forward_substitute([ratios_ref[k] for k in range(ratios_ref.shape[0])], image) * scale_ref[...]
    first = split_product(factor, [turned_ref[i] for i in range(3)], 0)
    last = split_product(factor, late, 1)
    for peer in range(out_ref.shape[0]):
        out_ref[peer, :, :split] = first
        out_ref[peer, :, split:] = last


def last_step(sums_ref, main_ref, late_ref, packed_ref):
    _, rank, rows = sums_ref.shape
    columns = main_ref.shape[2]
    value = total_of(sums_ref)
    packed_ref[:, :rows] = value
    image = split_product(
        value, [jnp.concatenate([main_ref[i], late_ref[i]], axis=0) for i in range(3)], 0
    )
    pivots, ratios = factorize(gram_of(value), image.shape)
    image = forward_substitute(ratios, image)
    packed_ref[:, rows:rows + columns] = back_substitute(ratios, image * (1.0 / pivots))
    packed_ref[:, rows + columns:] = image * (1.0 / jnp.sqrt(pivots))


def update_left(main_ref, late_ref, packed_ref, new_ref):
    rows, columns = new_ref.shape
    weights = GOSSIP_RATE * packed_ref[:, rows:rows + columns]
    start = 0
    for matrix_ref in (main_ref, late_ref):
        piece = pl.ds(start, matrix_ref.shape[0])
        new_ref[piece] = matrix_ref[...] + outer_product(packed_ref[:, piece], weights)
        start += matrix_ref.shape[0]


def update_right(matrix_ref, packed_ref, new_hbm, warm_hbm, new_vmem, warm_vmem, sems):
    rows, columns = matrix_ref.shape
    tile = rows // TILES
    warm_vmem[...] = packed_ref[:, rows + columns:]
    copies = [pltpu.make_async_copy(warm_vmem, warm_hbm.at[0], sems.at[TILES])]
    copies[0].start()
    weights = -GOSSIP_RATE * packed_ref[:, rows:rows + columns]
    for index in range(TILES):
        piece = pl.ds(index * tile, tile)
        new_vmem[piece] = matrix_ref[piece] + outer_product(packed_ref[:, piece], weights)
        copy = pltpu.make_async_copy(new_vmem.at[piece], new_hbm.at[0, piece], sems.at[index])
        copy.start()
        copies.append(copy)
    for copy in copies:
        copy.wait()


def sum_over_y(spread):
    peers = lax.axis_size("tp")
    groups = [list(range(start, peers, 2)) for start in range(2)]
    spread = lax.all_to_all(spread, "tp", 0, 0, axis_index_groups=groups)
    _, rank, rows = spread.shape
    return kernel_call(
        add_up, jax.ShapeDtypeStruct((rank, rows), jnp.float32), spread.size, 4 * spread.size
    )(spread)


def per_device(params, warm):
    _, rows, columns = params.shape
    rank = warm.shape[1]
    peers = lax.axis_size("tp")
    count = lax.axis_size("blk")
    one = rank * rows * columns * 2
    block = rows * columns * 4
    f32 = jnp.float32
    to_right = [(i, (i + 1) % count) for i in range(count)]
    to_left = [(i, (i - 1) % count) for i in range(count)]
    split_at = rows // 16 * SIXTEENTHS
    run = count // RUNS
    ends = [run * (i + 1) - 1 for i in range(RUNS)]
    swap_ends = [(i, i) for i in range(count) if i not in ends]
    swap_ends += [(end, ends[index - 1]) for index, end in enumerate(ends)]
    in_run = [(i, i // run * run + (i + 1) % run) for i in range(count)]

    def spread(peers):
        return jax.ShapeDtypeStruct((peers, rank, rows), f32)

    def split(rows):
        return jax.ShapeDtypeStruct((3, rows, columns), jnp.bfloat16)

    def turned(rows):
        return jax.ShapeDtypeStruct((3, columns, rows), jnp.bfloat16)

    matrix = jax.ShapeDtypeStruct((rows, columns), f32)
    hbm = pl.BlockSpec(memory_space=pltpu.HBM)
    factor_scratch = pltpu.VMEM((rank, columns), f32)
    sems = pltpu.SemaphoreType.DMA((TILES + 1,))

    packed, parts, main, late = kernel_call(
        own_product,
        (
            jax.ShapeDtypeStruct((rank, rows + columns), f32), turned(rows),
            jax.ShapeDtypeStruct((split_at, columns), f32),
            jax.ShapeDtypeStruct((rows - split_at, columns), f32),
        ),
        6 * one, 2 * block, in_specs=[hbm, hbm], scratch_shapes=[factor_scratch, sems],
    )(pltpu.with_memory_space_constraint(warm, pltpu.HBM), pltpu.with_memory_space_constraint(params, pltpu.HBM))
    packed = lax.ppermute(packed, "blk", to_right)
    left_main = lax.ppermute(main, "blk", to_right)
    carried = lax.ppermute(late, "blk", swap_ends)
    sums = kernel_call(spread_first, spread(peers // 2), 450 * one, block)(packed, parts)
    sums = sum_over_y(sums)
    carried, sums = lax.optimization_barrier((carried, sums))
    left_late = lax.ppermute(carried, "blk", in_run)
    other = lax.ppermute(sums, "tp", [(i, i ^ 1) for i in range(peers)])
    delta_main, delta_turned = kernel_call(
        split_difference, (split(split_at), turned(split_at)), one // 64, 3 * block
    )(main, left_main)
    factor_shape = jax.ShapeDtypeStruct((rank, columns), f32)
    value, image, scale, ratios = kernel_call(
        middle_main,
        (
            jax.ShapeDtypeStruct((rank, rows - split_at), f32), factor_shape, factor_shape,
            jax.ShapeDtypeStruct((rank - 1, rank, columns), f32),
        ),
        6 * one, 2 * block,
    )(sums, other, delta_main)
    delta_late, sums = kernel_call(middle_late, (split(rows - split_at), spread(peers)), 6 * one, 2 * block)(
        value, image, scale, ratios, delta_turned, late, left_late
    )
    sums = lax.all_to_all(sums, "tp", 0, 0)
    own = kernel_call(
        last_step, jax.ShapeDtypeStruct((rank, rows + 2 * columns), f32), 6 * one, 2 * block
    )(sums, delta_main, delta_late)
    right = lax.ppermute(own, "blk", to_left)
    left_done = kernel_call(update_left, matrix, 6 * one, 2 * block)(main, late, own)
    new_params, next_warm = kernel_call(
        update_right,
        (jax.ShapeDtypeStruct(params.shape, f32), jax.ShapeDtypeStruct(warm.shape, f32)),
        6 * one, 2 * block, out_specs=(hbm, hbm),
        scratch_shapes=[pltpu.VMEM(matrix.shape, f32), factor_scratch, sems],
    )(left_done, right)
    return new_params, next_warm


def solution(mesh):
    spec = P("blk", None, "tp")
    return jax.shard_map(
        per_device, mesh=mesh, in_specs=(spec, spec), out_specs=(spec, spec), check_vma=False
    )
```

profile of v0, /device:TPU:2, one launch (start us, length us, event | category | flops | bytes accessed | tf_op | source)
XLA Modules:
  0.0 68.9 jit_solution(10776918311383847169)
XLA Ops:
  0.6 2.4 %shard_map.41 = (f32[8,4224]{1,0:T(8,128)S(1)}, bf16[3,128,4096]{2,1,0:T(8,128)(2,1)S(1)}, f32[2816,128]{1,0:T(8,128)S(1)}, f32[1280,128]{1,0:T(8,128)S(1)}) custom-call(f32[1,8,128]{2,1,0:T(8,128)} %q_hbm.1, f32[1,4096,128]{2,1,0:T(8,128)} %matrix_hbm.1), custom_call_target="tpu_custom_call" | custom-call | flops 50331648 | bytes 4194304 | tf_op jit(solution)/shard_map/pallas_call | solution.py:258
  3.1 1.9 %collective-permute-start.1 = (f32[8,4224]{1,0:T(8,128)S(1)}, f32[8,4224]{1,0:T(8,128)S(1)}, u32[]{:S(2)}, u32[]{:S(2)}) collective-permute-start(f32[8,4224]{1,0:T(8,128)S(1)} %get-tuple-element.18), channel_id=1, source_target_pairs={{0,8},{8,16},{16,24},{24,32},{32,40},{40,48},{48,56},{56,64},{64,7... | collective-permute-start | bytes 405512 | tf_op jit(solution)/shard_map/ppermute | solution.py:267
  5.0 3.9 %collective-permute-start.3 = (f32[2816,128]{1,0:T(8,128)S(1)}, f32[2816,128]{1,0:T(8,128)S(1)}, u32[]{:S(2)}, u32[]{:S(2)}) collective-permute-start(f32[2816,128]{1,0:T(8,128)S(1)} %get-tuple-element.16.mine_ref.main_ref), channel_id=1, source_target_pairs={{0,8},{8,16},{16,24},{24,32},{32,40},{40,48},{48,56},{56,64},{64,7... | collective-permute-start | bytes 4325384 | tf_op jit(solution)/shard_map/ppermute | solution.py:268
  8.9 0.7 %collective-permute-start = (f32[1280,128]{1,0:T(8,128)S(1)}, f32[1280,128]{1,0:T(8,128)S(1)}, u32[]{:S(2)}, u32[]{:S(2)}) collective-permute-start(f32[1280,128]{1,0:T(8,128)S(1)} %get-tuple-element.17.mine_ref.late_ref), channel_id=1, source_target_pairs={{0,0},{8,8},{16,16},{24,24},{32,32},{40,40},{48,48},{56,56},{64,64... | collective-permute-start | bytes 1966088 | tf_op jit(solution)/shard_map/ppermute | solution.py:269
  9.6 6.9 %collective-permute-done.1.packed_ref = f32[8,4224]{1,0:T(8,128)S(1)} collective-permute-done((f32[8,4224]{1,0:T(8,128)S(1)}, f32[8,4224]{1,0:T(8,128)S(1)}, u32[]{:S(2)}, u32[]{:S(2)}) %collective-permute-start.1) | collective-permute-done | bytes 135200 | tf_op jit(solution)/shard_map/ppermute | solution.py:267
  16.6 0.5 shard_map.42
  17.1 12.3 %all_to_all.10.sums_ref = f32[4,8,4096]{2,1,0:T(8,128)S(1)} all-to-all(f32[4,8,4096]{2,1,0:T(8,128)S(1)} %shard_map.42), channel_id=1, replica_groups={{0,2,4,6},{1,3,5,7},{8,10,12,14},{9,11,13,15},{16,18,20,22},{17,19,21,2..., dimensions={0} | all-to-all | bytes 1048576 | tf_op jit(solution)/shard_map/all_to_all | solution.py:220
  29.5 0.0 collective-permute-done
  29.5 0.0 collective-permute-start.4
  29.5 4.3 %collective-permute-start.2 = (f32[8,4096]{1,0:T(8,128)S(1)}, f32[8,4096]{1,0:T(8,128)S(1)}, u32[]{:S(2)}, u32[]{:S(2)}) collective-permute-start(f32[8,4096]{1,0:T(8,128)S(1)} %shard_map.43.sum_ref), channel_id=1, source_target_pairs={{0,1},{1,0},{2,3},{3,2},{4,5},{5,4},{6,7},{7,6},{8,9},{9,8},{10,11... | collective-permute-start | bytes 393224 | tf_op jit(solution)/shard_map/ppermute | solution.py:274
  33.8 0.0 collective-permute-done.3.left_ref
  33.9 0.6 shard_map.44
  34.5 3.4 %collective-permute-done.2.other_ref = f32[8,4096]{1,0:T(8,128)S(1)} collective-permute-done((f32[8,4096]{1,0:T(8,128)S(1)}, f32[8,4096]{1,0:T(8,128)S(1)}, u32[]{:S(2)}, u32[]{:S(2)}) %collective-permute-start.2) | collective-permute-done | bytes 131104 | tf_op jit(solution)/shard_map/ppermute | solution.py:274
  37.9 0.7 %shard_map.45 = (f32[8,1280]{1,0:T(8,128)S(1)}, f32[8,128]{1,0:T(8,128)S(1)}, f32[8,128]{1,0:T(8,128)S(1)}, f32[7,8,128]{2,1,0:T(8,128)S(1)}) custom-call(f32[8,4096]{1,0:T(8,128)S(1)} %shard_map.43.sum_ref, f32[8,4096]{1,0:T(8,128)S(1)} %collective-permute-done.2.other_ref, bf16[3,2816,128]{2,1,0:T(8,128)(2,1)S(1)} %get-tuple-element.21.main_ref), custom_call_target="tpu_custom_call" | custom-call | flops 50331648 | bytes 4194304 | tf_op jit(solution)/shard_map/pallas_call | solution.py:279
  38.6 2.1 %collective-permute-done.4.left_ref = f32[1280,128]{1,0:T(8,128)S(1)} collective-permute-done((f32[1280,128]{1,0:T(8,128)S(1)}, f32[1280,128]{1,0:T(8,128)S(1)}, u32[]{:S(2)}, u32[]{:S(2)}) %collective-permute-start.4) | collective-permute-done | bytes 655392 | tf_op jit(solution)/shard_map/ppermute | solution.py:273
  40.7 1.0 %shard_map.46 = (bf16[3,1280,128]{2,1,0:T(8,128)(2,1)S(1)}, f32[8,8,4096]{2,1,0:T(8,128)S(1)}) custom-call(f32[8,1280]{1,0:T(8,128)S(1)} %get-tuple-element.22.value_ref, f32[8,128]{1,0:T(8,128)S(1)} %get-tuple-element.23.image_ref, f32[8,128]{1,0:T(8,128)S(1)} %get-tuple-element.24.scale_ref, f32[7,8,128]{2,1,0:T(8,128)S(1)} %get-tuple-element.25.ratios_ref, ...), custom_call_target="tpu_custom_call" | custom-call | flops 50331648 | bytes 4194304 | tf_op jit(solution)/shard_map/pallas_call | solution.py:287
  41.8 18.6 %all_to_all.11.sums_ref = f32[8,8,4096]{2,1,0:T(8,128)S(1)} all-to-all(f32[8,8,4096]{2,1,0:T(8,128)S(1)} %get-tuple-element.28), channel_id=1, replica_groups=mesh['blk'=64,'tp'=8] {'tp'}, dimensions={0} | all-to-all | bytes 2097152 | tf_op jit(solution)/shard_map/all_to_all | solution.py:290
  60.3 0.9 %shard_map.47.packed_ref = f32[8,4352]{1,0:T(8,128)S(1)} custom-call(f32[8,8,4096]{2,1,0:T(8,128)S(1)} %all_to_all.11.sums_ref, bf16[3,2816,128]{2,1,0:T(8,128)(2,1)S(1)} %get-tuple-element.21.main_ref, bf16[3,1280,128]{2,1,0:T(8,128)(2,1)S(1)} %get-tuple-element.29.late_ref), custom_call_target="tpu_custom_call" | custom-call | flops 50331648 | bytes 4194304 | tf_op jit(solution)/shard_map/pallas_call | solution.py:291
  61.2 3.4 %collective-permute-start.5 = (f32[8,4352]{1,0:T(8,128)S(1)}, f32[8,4352]{1,0:T(8,128)S(1)}, u32[]{:S(2)}, u32[]{:S(2)}) collective-permute-start(f32[8,4352]{1,0:T(8,128)S(1)} %shard_map.47.packed_ref), channel_id=1, source_target_pairs={{0,504},{8,0},{16,8},{24,16},{32,24},{40,32},{48,40},{56,48},{64,5... | collective-permute-start | bytes 417800 | tf_op jit(solution)/shard_map/ppermute | solution.py:294
  64.6 0.5 shard_map.48.matrix_ref
  65.1 2.1 %collective-permute-done.5.packed_ref = f32[8,4352]{1,0:T(8,128)S(1)} collective-permute-done((f32[8,4352]{1,0:T(8,128)S(1)}, f32[8,4352]{1,0:T(8,128)S(1)}, u32[]{:S(2)}, u32[]{:S(2)}) %collective-permute-start.5) | collective-permute-done | bytes 139296 | tf_op jit(solution)/shard_map/ppermute | solution.py:294
  67.2 1.7 %shard_map.49 = (f32[1,4096,128]{2,1,0:T(8,128)}, f32[1,8,128]{2,1,0:T(8,128)}) custom-call(f32[4096,128]{1,0:T(8,128)S(1)} %shard_map.48.matrix_ref, f32[8,4352]{1,0:T(8,128)S(1)} %collective-permute-done.5.packed_ref), custom_call_target="tpu_custom_call" | custom-call | flops 50331648 | bytes 4194304 | tf_op jit(solution)/shard_map/pallas_call | solution.py:296
  (1 shorter events, 0.0 us)
Async XLA Ops:
  3.1 13.5 %collective-permute-start.1 = (f32[8,4224]{1,0:T(8,128)S(1)}, f32[8,4224]{1,0:T(8,128)S(1)}, u32[]{:S(2)}, u32[]{:S(2)}) collective-permute-start(f32[8,4224]{1,0:T(8,128)S(1)} %get-tuple-element.18), channel_id=1, source_target_pairs={{0,8},{8,16},{16,24},{24,32},{32,40},{40,48},{48,56},{56,64},{64,7... | collective-permute-start | bytes 405512 | tf_op jit(solution)/shard_map/ppermute | solution.py:267
  5.0 28.9 %collective-permute-start.3 = (f32[2816,128]{1,0:T(8,128)S(1)}, f32[2816,128]{1,0:T(8,128)S(1)}, u32[]{:S(2)}, u32[]{:S(2)}) collective-permute-start(f32[2816,128]{1,0:T(8,128)S(1)} %get-tuple-element.16.mine_ref.main_ref), channel_id=1, source_target_pairs={{0,8},{8,16},{16,24},{24,32},{32,40},{40,48},{48,56},{56,64},{64,7... | collective-permute-start | bytes 4325384 | tf_op jit(solution)/shard_map/ppermute | solution.py:268
  8.9 20.6 %collective-permute-start = (f32[1280,128]{1,0:T(8,128)S(1)}, f32[1280,128]{1,0:T(8,128)S(1)}, u32[]{:S(2)}, u32[]{:S(2)}) collective-permute-start(f32[1280,128]{1,0:T(8,128)S(1)} %get-tuple-element.17.mine_ref.late_ref), channel_id=1, source_target_pairs={{0,0},{8,8},{16,16},{24,24},{32,32},{40,40},{48,48},{56,56},{64,64... | collective-permute-start | bytes 1966088 | tf_op jit(solution)/shard_map/ppermute | solution.py:269
  29.5 11.2 %collective-permute-start.4 = (f32[1280,128]{1,0:T(8,128)S(1)}, f32[1280,128]{1,0:T(8,128)S(1)}, u32[]{:S(2)}, u32[]{:S(2)}) collective-permute-start(f32[1280,128]{1,0:T(8,128)S(1)} %collective-permute-done), channel_id=1, source_target_pairs={{0,8},{8,16},{16,24},{24,32},{32,40},{40,48},{48,56},{56,64},{64,7... | collective-permute-start | bytes 1966088 | tf_op jit(solution)/shard_map/ppermute | solution.py:273
  29.5 8.4 %collective-permute-start.2 = (f32[8,4096]{1,0:T(8,128)S(1)}, f32[8,4096]{1,0:T(8,128)S(1)}, u32[]{:S(2)}, u32[]{:S(2)}) collective-permute-start(f32[8,4096]{1,0:T(8,128)S(1)} %shard_map.43.sum_ref), channel_id=1, source_target_pairs={{0,1},{1,0},{2,3},{3,2},{4,5},{5,4},{6,7},{7,6},{8,9},{9,8},{10,11... | collective-permute-start | bytes 393224 | tf_op jit(solution)/shard_map/ppermute | solution.py:274
  61.2 6.0 %collective-permute-start.5 = (f32[8,4352]{1,0:T(8,128)S(1)}, f32[8,4352]{1,0:T(8,128)S(1)}, u32[]{:S(2)}, u32[]{:S(2)}) collective-permute-start(f32[8,4352]{1,0:T(8,128)S(1)} %shard_map.47.packed_ref), channel_id=1, source_target_pairs={{0,504},{8,0},{16,8},{24,16},{32,24},{40,32},{48,40},{56,48},{64,5... | collective-permute-start | bytes 417800 | tf_op jit(solution)/shard_map/ppermute | solution.py:294
where the time goes:
time: 69.2 us; the launch traced here: 68.9 us
  blocking collectives  30.9 us (45%)
  waiting for transfers between devices  14.5 us (21%)
  starting transfers between devices  14.3 us (21%)
  Pallas kernels  8.49 us (12%)
  between operations  0.74 us (1%)
    all_to_all x1, blocking collectives, per_device(): sums = lax.all_to_all(sums, 'tp', 0, 0)  18.6 us
    all_to_all x1, blocking collectives, sum_over_y(): spread = lax.all_to_all(spread, 'tp', 0, 0, axis_index_groups=groups)  12.3 us
    ppermute x1, waiting for transfers between devices, per_device(): packed = lax.ppermute(packed, 'blk', to_right)  6.93 us
    ppermute x1, starting transfers between devices, per_device(): other = lax.ppermute(sums, 'tp', [(i, i ^ 1) for i in range(peers)])  4.33 us
    ppermute x1, starting transfers between devices, per_device(): left_main = lax.ppermute(main, 'blk', to_right)  3.93 us
    ppermute x1, starting transfers between devices, per_device(): right = lax.ppermute(own, 'blk', to_left)  3.37 us
    ppermute x1, waiting for transfers between devices, per_device(): other = lax.ppermute(sums, 'tp', [(i, i ^ 1) for i in range(peers)])  3.37 us
    pallas_call x1, Pallas kernels, per_device(): kernel_call(own_product, (jax.ShapeDtypeStruct((rank, rows + columns), f3...  2.42 us
  transfers between devices with their start and end apart: 6, of which 4 were waited for; matrix products, arithmetic and copies ran while one was open for 0% of the time, Pallas kernels for 3%

commit v1 on v0

--- a/solution.py
+++ b/solution.py
@@ -199,13 +199,13 @@
 
 def update_right(matrix_ref, packed_ref, new_hbm, warm_hbm, new_vmem, warm_vmem, sems):
     rows, columns = matrix_ref.shape
-    tile = rows // TILES
+    bounds = (0, rows // 8, rows // 2, rows)
     warm_vmem[...] = packed_ref[:, rows + columns:]
     copies = [pltpu.make_async_copy(warm_vmem, warm_hbm.at[0], sems.at[TILES])]
     copies[0].start()
     weights = -GOSSIP_RATE * packed_ref[:, rows:rows + columns]
-    for index in range(TILES):
-        piece = pl.ds(index * tile, tile)
+    for index, (start, end) in enumerate(zip(bounds, bounds[1:])):
+        piece = pl.ds(start, end - start)
         new_vmem[piece] = matrix_ref[piece] + outer_product(packed_ref[:, piece], weights)
         copy = pltpu.make_async_copy(new_vmem.at[piece], new_hbm.at[0, piece], sems.at[index])
         copy.start()

time: 69.2 us -> 69.4 us (level)
  no operation moved by 1% of the time
where the time goes in v1:
time: 69.4 us; the launch traced here: 69 us
  blocking collectives  30.9 us (45%)
  waiting for transfers between devices  14.5 us (21%)
  starting transfers between devices  14.3 us (21%)
  Pallas kernels  8.6 us (12%)
  between operations  0.74 us (1%)
    all_to_all x1, blocking collectives, per_device(): sums = lax.all_to_all(sums, 'tp', 0, 0)  18.6 us
    all_to_all x1, blocking collectives, sum_over_y(): spread = lax.all_to_all(spread, 'tp', 0, 0, axis_index_groups=groups)  12.3 us
    ppermute x1, waiting for transfers between devices, per_device(): packed = lax.ppermute(packed, 'blk', to_right)  6.93 us
    ppermute x1, starting transfers between devices, per_device(): other = lax.ppermute(sums, 'tp', [(i, i ^ 1) for i in range(peers)])  4.33 us
    ppermute x1, starting transfers between devices, per_device(): left_main = lax.ppermute(main, 'blk', to_right)  3.93 us
    ppermute x1, starting transfers between devices, per_device(): right = lax.ppermute(own, 'blk', to_left)  3.37 us
    ppermute x1, waiting for transfers between devices, per_device(): other = lax.ppermute(sums, 'tp', [(i, i ^ 1) for i in range(peers)])  3.37 us
    pallas_call x1, Pallas kernels, per_device(): kernel_call(own_product, (jax.ShapeDtypeStruct((rank, rows + columns), f3...  2.42 us
  transfers between devices with their start and end apart: 6, of which 4 were waited for; matrix products, arithmetic and copies ran while one was open for 0% of the time, Pallas kernels for 3%

profile of v1, /device:TPU:2, one launch (start us, length us, event | category | flops | bytes accessed | tf_op | source)
XLA Modules:
  0.0 69.0 jit_solution(9440162660666645197)
XLA Ops:
  0.6 2.4 %shard_map.41 = (f32[8,4224]{1,0:T(8,128)S(1)}, bf16[3,128,4096]{2,1,0:T(8,128)(2,1)S(1)}, f32[2816,128]{1,0:T(8,128)S(1)}, f32[1280,128]{1,0:T(8,128)S(1)}) custom-call(f32[1,8,128]{2,1,0:T(8,128)} %q_hbm.1, f32[1,4096,128]{2,1,0:T(8,128)} %matrix_hbm.1), custom_call_target="tpu_custom_call" | custom-call | flops 50331648 | bytes 4194304 | tf_op jit(solution)/shard_map/pallas_call | solution.py:258
  3.1 1.9 %collective-permute-start.1 = (f32[8,4224]{1,0:T(8,128)S(1)}, f32[8,4224]{1,0:T(8,128)S(1)}, u32[]{:S(2)}, u32[]{:S(2)}) collective-permute-start(f32[8,4224]{1,0:T(8,128)S(1)} %get-tuple-element.18), channel_id=1, source_target_pairs={{0,8},{8,16},{16,24},{24,32},{32,40},{40,48},{48,56},{56,64},{64,7... | collective-permute-start | bytes 405512 | tf_op jit(solution)/shard_map/ppermute | solution.py:267
  5.0 3.9 %collective-permute-start.3 = (f32[2816,128]{1,0:T(8,128)S(1)}, f32[2816,128]{1,0:T(8,128)S(1)}, u32[]{:S(2)}, u32[]{:S(2)}) collective-permute-start(f32[2816,128]{1,0:T(8,128)S(1)} %get-tuple-element.16.mine_ref.main_ref), channel_id=1, source_target_pairs={{0,8},{8,16},{16,24},{24,32},{32,40},{40,48},{48,56},{56,64},{64,7... | collective-permute-start | bytes 4325384 | tf_op jit(solution)/shard_map/ppermute | solution.py:268
  8.9 0.7 %collective-permute-start = (f32[1280,128]{1,0:T(8,128)S(1)}, f32[1280,128]{1,0:T(8,128)S(1)}, u32[]{:S(2)}, u32[]{:S(2)}) collective-permute-start(f32[1280,128]{1,0:T(8,128)S(1)} %get-tuple-element.17.mine_ref.late_ref), channel_id=1, source_target_pairs={{0,0},{8,8},{16,16},{24,24},{32,32},{40,40},{48,48},{56,56},{64,64... | collective-permute-start | bytes 1966088 | tf_op jit(solution)/shard_map/ppermute | solution.py:269
  9.6 6.9 %collective-permute-done.1.packed_ref = f32[8,4224]{1,0:T(8,128)S(1)} collective-permute-done((f32[8,4224]{1,0:T(8,128)S(1)}, f32[8,4224]{1,0:T(8,128)S(1)}, u32[]{:S(2)}, u32[]{:S(2)}) %collective-permute-start.1) | collective-permute-done | bytes 135200 | tf_op jit(solution)/shard_map/ppermute | solution.py:267
  16.6 0.5 shard_map.42
  17.1 12.3 %all_to_all.10.sums_ref = f32[4,8,4096]{2,1,0:T(8,128)S(1)} all-to-all(f32[4,8,4096]{2,1,0:T(8,128)S(1)} %shard_map.42), channel_id=1, replica_groups={{0,2,4,6},{1,3,5,7},{8,10,12,14},{9,11,13,15},{16,18,20,22},{17,19,21,2..., dimensions={0} | all-to-all | bytes 1048576 | tf_op jit(solution)/shard_map/all_to_all | solution.py:220
  29.5 0.0 collective-permute-done
  29.5 0.0 collective-permute-start.4
  29.5 4.3 %collective-permute-start.2 = (f32[8,4096]{1,0:T(8,128)S(1)}, f32[8,4096]{1,0:T(8,128)S(1)}, u32[]{:S(2)}, u32[]{:S(2)}) collective-permute-start(f32[8,4096]{1,0:T(8,128)S(1)} %shard_map.43.sum_ref), channel_id=1, source_target_pairs={{0,1},{1,0},{2,3},{3,2},{4,5},{5,4},{6,7},{7,6},{8,9},{9,8},{10,11... | collective-permute-start | bytes 393224 | tf_op jit(solution)/shard_map/ppermute | solution.py:274
  33.8 0.0 collective-permute-done.3.left_ref
  33.9 0.6 shard_map.44
  34.5 3.4 %collective-permute-done.2.other_ref = f32[8,4096]{1,0:T(8,128)S(1)} collective-permute-done((f32[8,4096]{1,0:T(8,128)S(1)}, f32[8,4096]{1,0:T(8,128)S(1)}, u32[]{:S(2)}, u32[]{:S(2)}) %collective-permute-start.2) | collective-permute-done | bytes 131104 | tf_op jit(solution)/shard_map/ppermute | solution.py:274
  37.9 0.7 %shard_map.45 = (f32[8,1280]{1,0:T(8,128)S(1)}, f32[8,128]{1,0:T(8,128)S(1)}, f32[8,128]{1,0:T(8,128)S(1)}, f32[7,8,128]{2,1,0:T(8,128)S(1)}) custom-call(f32[8,4096]{1,0:T(8,128)S(1)} %shard_map.43.sum_ref, f32[8,4096]{1,0:T(8,128)S(1)} %collective-permute-done.2.other_ref, bf16[3,2816,128]{2,1,0:T(8,128)(2,1)S(1)} %get-tuple-element.21.main_ref), custom_call_target="tpu_custom_call" | custom-call | flops 50331648 | bytes 4194304 | tf_op jit(solution)/shard_map/pallas_call | solution.py:279
  38.6 2.1 %collective-permute-done.4.left_ref = f32[1280,128]{1,0:T(8,128)S(1)} collective-permute-done((f32[1280,128]{1,0:T(8,128)S(1)}, f32[1280,128]{1,0:T(8,128)S(1)}, u32[]{:S(2)}, u32[]{:S(2)}) %collective-permute-start.4) | collective-permute-done | bytes 655392 | tf_op jit(solution)/shard_map/ppermute | solution.py:273
  40.7 1.0 %shard_map.46 = (bf16[3,1280,128]{2,1,0:T(8,128)(2,1)S(1)}, f32[8,8,4096]{2,1,0:T(8,128)S(1)}) custom-call(f32[8,1280]{1,0:T(8,128)S(1)} %get-tuple-element.22.value_ref, f32[8,128]{1,0:T(8,128)S(1)} %get-tuple-element.23.image_ref, f32[8,128]{1,0:T(8,128)S(1)} %get-tuple-element.24.scale_ref, f32[7,8,128]{2,1,0:T(8,128)S(1)} %get-tuple-element.25.ratios_ref, ...), custom_call_target="tpu_custom_call" | custom-call | flops 50331648 | bytes 4194304 | tf_op jit(solution)/shard_map/pallas_call | solution.py:287
  41.8 18.6 %all_to_all.11.sums_ref = f32[8,8,4096]{2,1,0:T(8,128)S(1)} all-to-all(f32[8,8,4096]{2,1,0:T(8,128)S(1)} %get-tuple-element.28), channel_id=1, replica_groups=mesh['blk'=64,'tp'=8] {'tp'}, dimensions={0} | all-to-all | bytes 2097152 | tf_op jit(solution)/shard_map/all_to_all | solution.py:290
  60.3 0.9 %shard_map.47.packed_ref = f32[8,4352]{1,0:T(8,128)S(1)} custom-call(f32[8,8,4096]{2,1,0:T(8,128)S(1)} %all_to_all.11.sums_ref, bf16[3,2816,128]{2,1,0:T(8,128)(2,1)S(1)} %get-tuple-element.21.main_ref, bf16[3,1280,128]{2,1,0:T(8,128)(2,1)S(1)} %get-tuple-element.29.late_ref), custom_call_target="tpu_custom_call" | custom-call | flops 50331648 | bytes 4194304 | tf_op jit(solution)/shard_map/pallas_call | solution.py:291
  61.2 3.4 %collective-permute-start.5 = (f32[8,4352]{1,0:T(8,128)S(1)}, f32[8,4352]{1,0:T(8,128)S(1)}, u32[]{:S(2)}, u32[]{:S(2)}) collective-permute-start(f32[8,4352]{1,0:T(8,128)S(1)} %shard_map.47.packed_ref), channel_id=1, source_target_pairs={{0,504},{8,0},{16,8},{24,16},{32,24},{40,32},{48,40},{56,48},{64,5... | collective-permute-start | bytes 417800 | tf_op jit(solution)/shard_map/ppermute | solution.py:294
  64.6 0.5 shard_map.48.matrix_ref
  65.1 2.1 %collective-permute-done.5.packed_ref = f32[8,4352]{1,0:T(8,128)S(1)} collective-permute-done((f32[8,4352]{1,0:T(8,128)S(1)}, f32[8,4352]{1,0:T(8,128)S(1)}, u32[]{:S(2)}, u32[]{:S(2)}) %collective-permute-start.5) | collective-permute-done | bytes 139296 | tf_op jit(solution)/shard_map/ppermute | solution.py:294
  67.2 1.8 %shard_map.49 = (f32[1,4096,128]{2,1,0:T(8,128)}, f32[1,8,128]{2,1,0:T(8,128)}) custom-call(f32[4096,128]{1,0:T(8,128)S(1)} %shard_map.48.matrix_ref, f32[8,4352]{1,0:T(8,128)S(1)} %collective-permute-done.5.packed_ref), custom_call_target="tpu_custom_call" | custom-call | flops 50331648 | bytes 4194304 | tf_op jit(solution)/shard_map/pallas_call | solution.py:296
  (1 shorter events, 0.0 us)
Async XLA Ops:
  3.1 13.5 %collective-permute-start.1 = (f32[8,4224]{1,0:T(8,128)S(1)}, f32[8,4224]{1,0:T(8,128)S(1)}, u32[]{:S(2)}, u32[]{:S(2)}) collective-permute-start(f32[8,4224]{1,0:T(8,128)S(1)} %get-tuple-element.18), channel_id=1, source_target_pairs={{0,8},{8,16},{16,24},{24,32},{32,40},{40,48},{48,56},{56,64},{64,7... | collective-permute-start | bytes 405512 | tf_op jit(solution)/shard_map/ppermute | solution.py:267
  5.0 28.9 %collective-permute-start.3 = (f32[2816,128]{1,0:T(8,128)S(1)}, f32[2816,128]{1,0:T(8,128)S(1)}, u32[]{:S(2)}, u32[]{:S(2)}) collective-permute-start(f32[2816,128]{1,0:T(8,128)S(1)} %get-tuple-element.16.mine_ref.main_ref), channel_id=1, source_target_pairs={{0,8},{8,16},{16,24},{24,32},{32,40},{40,48},{48,56},{56,64},{64,7... | collective-permute-start | bytes 4325384 | tf_op jit(solution)/shard_map/ppermute | solution.py:268
  8.9 20.6 %collective-permute-start = (f32[1280,128]{1,0:T(8,128)S(1)}, f32[1280,128]{1,0:T(8,128)S(1)}, u32[]{:S(2)}, u32[]{:S(2)}) collective-permute-start(f32[1280,128]{1,0:T(8,128)S(1)} %get-tuple-element.17.mine_ref.late_ref), channel_id=1, source_target_pairs={{0,0},{8,8},{16,16},{24,24},{32,32},{40,40},{48,48},{56,56},{64,64... | collective-permute-start | bytes 1966088 | tf_op jit(solution)/shard_map/ppermute | solution.py:269
  29.5 11.2 %collective-permute-start.4 = (f32[1280,128]{1,0:T(8,128)S(1)}, f32[1280,128]{1,0:T(8,128)S(1)}, u32[]{:S(2)}, u32[]{:S(2)}) collective-permute-start(f32[1280,128]{1,0:T(8,128)S(1)} %collective-permute-done), channel_id=1, source_target_pairs={{0,8},{8,16},{16,24},{24,32},{32,40},{40,48},{48,56},{56,64},{64,7... | collective-permute-start | bytes 1966088 | tf_op jit(solution)/shard_map/ppermute | solution.py:273
  29.5 8.4 %collective-permute-start.2 = (f32[8,4096]{1,0:T(8,128)S(1)}, f32[8,4096]{1,0:T(8,128)S(1)}, u32[]{:S(2)}, u32[]{:S(2)}) collective-permute-start(f32[8,4096]{1,0:T(8,128)S(1)} %shard_map.43.sum_ref), channel_id=1, source_target_pairs={{0,1},{1,0},{2,3},{3,2},{4,5},{5,4},{6,7},{7,6},{8,9},{9,8},{10,11... | collective-permute-start | bytes 393224 | tf_op jit(solution)/shard_map/ppermute | solution.py:274
  61.2 6.0 %collective-permute-start.5 = (f32[8,4352]{1,0:T(8,128)S(1)}, f32[8,4352]{1,0:T(8,128)S(1)}, u32[]{:S(2)}, u32[]{:S(2)}) collective-permute-start(f32[8,4352]{1,0:T(8,128)S(1)} %shard_map.47.packed_ref), channel_id=1, source_target_pairs={{0,504},{8,0},{16,8},{24,16},{32,24},{40,32},{48,40},{56,48},{64,5... | collective-permute-start | bytes 417800 | tf_op jit(solution)/shard_map/ppermute | solution.py:294

commit v2 on v0

--- a/solution.py
+++ b/solution.py
@@ -7,7 +7,7 @@
 
 GOSSIP_RATE = 0.5
 TILES = 4
-SIXTEENTHS = 11
+DIRECT = 23
 RUNS = 2
 
 
@@ -234,7 +234,7 @@
     f32 = jnp.float32
     to_right = [(i, (i + 1) % count) for i in range(count)]
     to_left = [(i, (i - 1) % count) for i in range(count)]
-    split_at = rows // 16 * SIXTEENTHS
+    split_at = rows // 32 * DIRECT
     run = count // RUNS
     ends = [run * (i + 1) - 1 for i in range(RUNS)]
     swap_ends = [(i, i) for i in range(count) if i not in ends]
@@ -267,7 +267,7 @@
     packed = lax.ppermute(packed, "blk", to_right)
     left_main = lax.ppermute(main, "blk", to_right)
     carried = lax.ppermute(late, "blk", swap_ends)
-    sums = kernel_call(spread_first, spread(peers // 2), 450 * one, block)(packed, parts)
+    sums = kernel_call(spread_first, spread(peers // 2), 600 * one, block)(packed, parts)
     sums = sum_over_y(sums)
     carried, sums = lax.optimization_barrier((carried, sums))
     left_late = lax.ppermute(carried, "blk", in_run)

time: 69.2 us -> 69.5 us (level)
  blocking collectives: 30.9 us -> 32.9 us
  starting transfers between devices: 14.3 us -> 13 us
  waiting for transfers between devices: 14.5 us -> 13.8 us
    all_to_all x1, blocking collectives: 18.6 us -> 20.6 us  [per_device(): sums = lax.all_to_all(sums, 'tp', 0, 0)]
    ppermute x1, starting transfers between devices: 3.37 us -> 2.09 us  [per_device(): right = lax.ppermute(own, 'blk', to_left)]
    ppermute x1, waiting for transfers between devices: 2.13 us -> 1.39 us  [per_device(): left_late = lax.ppermute(carried, 'blk', in_run)]
  transfers between devices with their start and end apart: 6 -> 6, of which waited for: 4 -> 4; matrix products, arithmetic and copies ran while one was open for 0% -> 0% of each run, Pallas kernels for 3% -> 4%
where the time goes in v2:
time: 69.5 us; the launch traced here: 69 us
  blocking collectives  32.9 us (47%)
  waiting for transfers between devices  13.8 us (20%)
  starting transfers between devices  13 us (19%)
  Pallas kernels  8.64 us (12%)
  between operations  0.74 us (1%)
    all_to_all x1, blocking collectives, per_device(): sums = lax.all_to_all(sums, 'tp', 0, 0)  20.6 us
    all_to_all x1, blocking collectives, sum_over_y(): spread = lax.all_to_all(spread, 'tp', 0, 0, axis_index_groups=groups)  12.3 us
    ppermute x1, waiting for transfers between devices, per_device(): packed = lax.ppermute(packed, 'blk', to_right)  6.93 us
    ppermute x1, starting transfers between devices, per_device(): other = lax.ppermute(sums, 'tp', [(i, i ^ 1) for i in range(peers)])  4.33 us
    ppermute x1, starting transfers between devices, per_device(): left_main = lax.ppermute(main, 'blk', to_right)  3.93 us
    ppermute x1, waiting for transfers between devices, per_device(): other = lax.ppermute(sums, 'tp', [(i, i ^ 1) for i in range(peers)])  3.33 us
    pallas_call x1, Pallas kernels, per_device(): kernel_call(own_product, (jax.ShapeDtypeStruct((rank, rows + columns), f3...  2.46 us
    ppermute x1, starting transfers between devices, per_device(): right = lax.ppermute(own, 'blk', to_left)  2.09 us
  transfers between devices with their start and end apart: 6, of which 4 were waited for; matrix products, arithmetic and copies ran while one was open for 0% of the time, Pallas kernels for 4%

profile of v2, /device:TPU:2, one launch (start us, length us, event | category | flops | bytes accessed | tf_op | source)
XLA Modules:
  0.0 69.0 jit_solution(15148903695371384777)
XLA Ops:
  0.6 2.5 %shard_map.41 = (f32[8,4224]{1,0:T(8,128)S(1)}, bf16[3,128,4096]{2,1,0:T(8,128)(2,1)S(1)}, f32[2944,128]{1,0:T(8,128)S(1)}, f32[1152,128]{1,0:T(8,128)S(1)}) custom-call(f32[1,8,128]{2,1,0:T(8,128)} %q_hbm.1, f32[1,4096,128]{2,1,0:T(8,128)} %matrix_hbm.1), custom_call_target="tpu_custom_call" | custom-call | flops 50331648 | bytes 4194304 | tf_op jit(solution)/shard_map/pallas_call | solution.py:258
  3.1 1.9 %collective-permute-start.1 = (f32[8,4224]{1,0:T(8,128)S(1)}, f32[8,4224]{1,0:T(8,128)S(1)}, u32[]{:S(2)}, u32[]{:S(2)}) collective-permute-start(f32[8,4224]{1,0:T(8,128)S(1)} %get-tuple-element.18), channel_id=1, source_target_pairs={{0,8},{8,16},{16,24},{24,32},{32,40},{40,48},{48,56},{56,64},{64,7... | collective-permute-start | bytes 405512 | tf_op jit(solution)/shard_map/ppermute | solution.py:267
  5.0 3.9 %collective-permute-start.3 = (f32[2944,128]{1,0:T(8,128)S(1)}, f32[2944,128]{1,0:T(8,128)S(1)}, u32[]{:S(2)}, u32[]{:S(2)}) collective-permute-start(f32[2944,128]{1,0:T(8,128)S(1)} %get-tuple-element.16.mine_ref.main_ref), channel_id=1, source_target_pairs={{0,8},{8,16},{16,24},{24,32},{32,40},{40,48},{48,56},{56,64},{64,7... | collective-permute-start | bytes 4521992 | tf_op jit(solution)/shard_map/ppermute | solution.py:268
  9.0 0.7 %collective-permute-start = (f32[1152,128]{1,0:T(8,128)S(1)}, f32[1152,128]{1,0:T(8,128)S(1)}, u32[]{:S(2)}, u32[]{:S(2)}) collective-permute-start(f32[1152,128]{1,0:T(8,128)S(1)} %get-tuple-element.17.mine_ref.late_ref), channel_id=1, source_target_pairs={{0,0},{8,8},{16,16},{24,24},{32,32},{40,40},{48,48},{56,56},{64,64... | collective-permute-start | bytes 1769480 | tf_op jit(solution)/shard_map/ppermute | solution.py:269
  9.7 6.9 %collective-permute-done.1.packed_ref = f32[8,4224]{1,0:T(8,128)S(1)} collective-permute-done((f32[8,4224]{1,0:T(8,128)S(1)}, f32[8,4224]{1,0:T(8,128)S(1)}, u32[]{:S(2)}, u32[]{:S(2)}) %collective-permute-start.1) | collective-permute-done | bytes 135200 | tf_op jit(solution)/shard_map/ppermute | solution.py:267
  16.6 0.5 shard_map.42
  17.1 12.3 %all_to_all.10.sums_ref = f32[4,8,4096]{2,1,0:T(8,128)S(1)} all-to-all(f32[4,8,4096]{2,1,0:T(8,128)S(1)} %shard_map.42), channel_id=1, replica_groups={{0,2,4,6},{1,3,5,7},{8,10,12,14},{9,11,13,15},{16,18,20,22},{17,19,21,2..., dimensions={0} | all-to-all | bytes 1048576 | tf_op jit(solution)/shard_map/all_to_all | solution.py:220
  29.5 0.0 collective-permute-done
  29.5 0.0 collective-permute-start.4
  29.6 4.3 %collective-permute-start.2 = (f32[8,4096]{1,0:T(8,128)S(1)}, f32[8,4096]{1,0:T(8,128)S(1)}, u32[]{:S(2)}, u32[]{:S(2)}) collective-permute-start(f32[8,4096]{1,0:T(8,128)S(1)} %shard_map.43.sum_ref), channel_id=1, source_target_pairs={{0,1},{1,0},{2,3},{3,2},{4,5},{5,4},{6,7},{7,6},{8,9},{9,8},{10,11... | collective-permute-start | bytes 393224 | tf_op jit(solution)/shard_map/ppermute | solution.py:274
  33.9 0.0 collective-permute-done.3.left_ref
  33.9 0.7 %shard_map.44 = (bf16[3,2944,128]{2,1,0:T(8,128)(2,1)S(1)}, bf16[3,128,2944]{2,1,0:T(8,128)(2,1)S(1)}) custom-call(f32[2944,128]{1,0:T(8,128)S(1)} %get-tuple-element.16.mine_ref.main_ref, f32[2944,128]{1,0:T(8,128)S(1)} %collective-permute-done.3.left_ref), custom_call_target="tpu_custom_call" | custom-call | flops 131072 | bytes 6291456 | tf_op jit(solution)/shard_map/pallas_call | solution.py:275
  34.6 3.3 %collective-permute-done.2.other_ref = f32[8,4096]{1,0:T(8,128)S(1)} collective-permute-done((f32[8,4096]{1,0:T(8,128)S(1)}, f32[8,4096]{1,0:T(8,128)S(1)}, u32[]{:S(2)}, u32[]{:S(2)}) %collective-permute-start.2) | collective-permute-done | bytes 131104 | tf_op jit(solution)/shard_map/ppermute | solution.py:274
  37.9 0.7 %shard_map.45 = (f32[8,1152]{1,0:T(8,128)S(1)}, f32[8,128]{1,0:T(8,128)S(1)}, f32[8,128]{1,0:T(8,128)S(1)}, f32[7,8,128]{2,1,0:T(8,128)S(1)}) custom-call(f32[8,4096]{1,0:T(8,128)S(1)} %shard_map.43.sum_ref, f32[8,4096]{1,0:T(8,128)S(1)} %collective-permute-done.2.other_ref, bf16[3,2944,128]{2,1,0:T(8,128)(2,1)S(1)} %get-tuple-element.21.main_ref), custom_call_target="tpu_custom_call" | custom-call | flops 50331648 | bytes 4194304 | tf_op jit(solution)/shard_map/pallas_call | solution.py:279
  38.7 1.4 %collective-permute-done.4.left_ref = f32[1152,128]{1,0:T(8,128)S(1)} collective-permute-done((f32[1152,128]{1,0:T(8,128)S(1)}, f32[1152,128]{1,0:T(8,128)S(1)}, u32[]{:S(2)}, u32[]{:S(2)}) %collective-permute-start.4) | collective-permute-done | bytes 589856 | tf_op jit(solution)/shard_map/ppermute | solution.py:273
  40.1 1.1 %shard_map.46 = (bf16[3,1152,128]{2,1,0:T(8,128)(2,1)S(1)}, f32[8,8,4096]{2,1,0:T(8,128)S(1)}) custom-call(f32[8,1152]{1,0:T(8,128)S(1)} %get-tuple-element.22.value_ref, f32[8,128]{1,0:T(8,128)S(1)} %get-tuple-element.23.image_ref, f32[8,128]{1,0:T(8,128)S(1)} %get-tuple-element.24.scale_ref, f32[7,8,128]{2,1,0:T(8,128)S(1)} %get-tuple-element.25.ratios_ref, ...), custom_call_target="tpu_custom_call" | custom-call | flops 50331648 | bytes 4194304 | tf_op jit(solution)/shard_map/pallas_call | solution.py:287
  41.1 20.6 %all_to_all.11.sums_ref = f32[8,8,4096]{2,1,0:T(8,128)S(1)} all-to-all(f32[8,8,4096]{2,1,0:T(8,128)S(1)} %get-tuple-element.28), channel_id=1, replica_groups=mesh['blk'=64,'tp'=8] {'tp'}, dimensions={0} | all-to-all | bytes 2097152 | tf_op jit(solution)/shard_map/all_to_all | solution.py:290
  61.7 0.9 %shard_map.47.packed_ref = f32[8,4352]{1,0:T(8,128)S(1)} custom-call(f32[8,8,4096]{2,1,0:T(8,128)S(1)} %all_to_all.11.sums_ref, bf16[3,2944,128]{2,1,0:T(8,128)(2,1)S(1)} %get-tuple-element.21.main_ref, bf16[3,1152,128]{2,1,0:T(8,128)(2,1)S(1)} %get-tuple-element.29.late_ref), custom_call_target="tpu_custom_call" | custom-call | flops 50331648 | bytes 4194304 | tf_op jit(solution)/shard_map/pallas_call | solution.py:291
  62.6 2.1 %collective-permute-start.5 = (f32[8,4352]{1,0:T(8,128)S(1)}, f32[8,4352]{1,0:T(8,128)S(1)}, u32[]{:S(2)}, u32[]{:S(2)}) collective-permute-start(f32[8,4352]{1,0:T(8,128)S(1)} %shard_map.47.packed_ref), channel_id=1, source_target_pairs={{0,504},{8,0},{16,8},{24,16},{32,24},{40,32},{48,40},{56,48},{64,5... | collective-permute-start | bytes 417800 | tf_op jit(solution)/shard_map/ppermute | solution.py:294
  64.7 0.5 shard_map.48.matrix_ref
  65.2 2.1 %collective-permute-done.5.packed_ref = f32[8,4352]{1,0:T(8,128)S(1)} collective-permute-done((f32[8,4352]{1,0:T(8,128)S(1)}, f32[8,4352]{1,0:T(8,128)S(1)}, u32[]{:S(2)}, u32[]{:S(2)}) %collective-permute-start.5) | collective-permute-done | bytes 139296 | tf_op jit(solution)/shard_map/ppermute | solution.py:294
  67.3 1.7 %shard_map.49 = (f32[1,4096,128]{2,1,0:T(8,128)}, f32[1,8,128]{2,1,0:T(8,128)}) custom-call(f32[4096,128]{1,0:T(8,128)S(1)} %shard_map.48.matrix_ref, f32[8,4352]{1,0:T(8,128)S(1)} %collective-permute-done.5.packed_ref), custom_call_target="tpu_custom_call" | custom-call | flops 50331648 | bytes 4194304 | tf_op jit(solution)/shard_map/pallas_call | solution.py:296
  (1 shorter events, 0.0 us)
Async XLA Ops:
  3.1 13.5 %collective-permute-start.1 = (f32[8,4224]{1,0:T(8,128)S(1)}, f32[8,4224]{1,0:T(8,128)S(1)}, u32[]{:S(2)}, u32[]{:S(2)}) collective-permute-start(f32[8,4224]{1,0:T(8,128)S(1)} %get-tuple-element.18), channel_id=1, source_target_pairs={{0,8},{8,16},{16,24},{24,32},{32,40},{40,48},{48,56},{56,64},{64,7... | collective-permute-start | bytes 405512 | tf_op jit(solution)/shard_map/ppermute | solution.py:267
  5.0 28.9 %collective-permute-start.3 = (f32[2944,128]{1,0:T(8,128)S(1)}, f32[2944,128]{1,0:T(8,128)S(1)}, u32[]{:S(2)}, u32[]{:S(2)}) collective-permute-start(f32[2944,128]{1,0:T(8,128)S(1)} %get-tuple-element.16.mine_ref.main_ref), channel_id=1, source_target_pairs={{0,8},{8,16},{16,24},{24,32},{32,40},{40,48},{48,56},{56,64},{64,7... | collective-permute-start | bytes 4521992 | tf_op jit(solution)/shard_map/ppermute | solution.py:268
  9.0 20.6 %collective-permute-start = (f32[1152,128]{1,0:T(8,128)S(1)}, f32[1152,128]{1,0:T(8,128)S(1)}, u32[]{:S(2)}, u32[]{:S(2)}) collective-permute-start(f32[1152,128]{1,0:T(8,128)S(1)} %get-tuple-element.17.mine_ref.late_ref), channel_id=1, source_target_pairs={{0,0},{8,8},{16,16},{24,24},{32,32},{40,40},{48,48},{56,56},{64,64... | collective-permute-start | bytes 1769480 | tf_op jit(solution)/shard_map/ppermute | solution.py:269
  29.5 10.5 %collective-permute-start.4 = (f32[1152,128]{1,0:T(8,128)S(1)}, f32[1152,128]{1,0:T(8,128)S(1)}, u32[]{:S(2)}, u32[]{:S(2)}) collective-permute-start(f32[1152,128]{1,0:T(8,128)S(1)} %collective-permute-done), channel_id=1, source_target_pairs={{0,8},{8,16},{16,24},{24,32},{32,40},{40,48},{48,56},{56,64},{64,7... | collective-permute-start | bytes 1769480 | tf_op jit(solution)/shard_map/ppermute | solution.py:273
  29.6 8.4 %collective-permute-start.2 = (f32[8,4096]{1,0:T(8,128)S(1)}, f32[8,4096]{1,0:T(8,128)S(1)}, u32[]{:S(2)}, u32[]{:S(2)}) collective-permute-start(f32[8,4096]{1,0:T(8,128)S(1)} %shard_map.43.sum_ref), channel_id=1, source_target_pairs={{0,1},{1,0},{2,3},{3,2},{4,5},{5,4},{6,7},{7,6},{8,9},{9,8},{10,11... | collective-permute-start | bytes 393224 | tf_op jit(solution)/shard_map/ppermute | solution.py:274
  62.6 4.7 %collective-permute-start.5 = (f32[8,4352]{1,0:T(8,128)S(1)}, f32[8,4352]{1,0:T(8,128)S(1)}, u32[]{:S(2)}, u32[]{:S(2)}) collective-permute-start(f32[8,4352]{1,0:T(8,128)S(1)} %shard_map.47.packed_ref), channel_id=1, source_target_pairs={{0,504},{8,0},{16,8},{24,16},{32,24},{40,32},{48,40},{56,48},{64,5... | collective-permute-start | bytes 417800 | tf_op jit(solution)/shard_map/ppermute | solution.py:294

commit v3 on v0

--- a/solution.py
+++ b/solution.py
@@ -214,14 +214,16 @@
         copy.wait()
 
 
-def sum_over_y(spread):
+def sum_over_y(spread, carried):
     peers = lax.axis_size("tp")
     groups = [list(range(start, peers, 2)) for start in range(2)]
     spread = lax.all_to_all(spread, "tp", 0, 0, axis_index_groups=groups)
+    carried, spread = lax.optimization_barrier((carried, spread))
     _, rank, rows = spread.shape
-    return kernel_call(
+    total = kernel_call(
         add_up, jax.ShapeDtypeStruct((rank, rows), jnp.float32), spread.size, 4 * spread.size
     )(spread)
+    return total, carried
 
 
 def per_device(params, warm):
@@ -268,8 +270,7 @@
     left_main = lax.ppermute(main, "blk", to_right)
     carried = lax.ppermute(late, "blk", swap_ends)
     sums = kernel_call(spread_first, spread(peers // 2), 450 * one, block)(packed, parts)
-    sums = sum_over_y(sums)
-    carried, sums = lax.optimization_barrier((carried, sums))
+    sums, carried = sum_over_y(sums, carried)
     left_late = lax.ppermute(carried, "blk", in_run)
     other = lax.ppermute(sums, "tp", [(i, i ^ 1) for i in range(peers)])
     delta_main, delta_turned = kernel_call(

time: 69.2 us -> 69.3 us (level)
  no operation moved by 1% of the time
where the time goes in v3:
time: 69.3 us; the launch traced here: 68.9 us
  blocking collectives  30.9 us (45%)
  waiting for transfers between devices  14.5 us (21%)
  starting transfers between devices  14.3 us (21%)
  Pallas kernels  8.49 us (12%)
  between operations  0.73 us (1%)
    all_to_all x1, blocking collectives, per_device(): sums = lax.all_to_all(sums, 'tp', 0, 0)  18.6 us
    all_to_all x1, blocking collectives, sum_over_y(): spread = lax.all_to_all(spread, 'tp', 0, 0, axis_index_groups=groups)  12.3 us
    ppermute x1, waiting for transfers between devices, per_device(): packed = lax.ppermute(packed, 'blk', to_right)  6.93 us
    ppermute x1, starting transfers between devices, per_device(): other = lax.ppermute(sums, 'tp', [(i, i ^ 1) for i in range(peers)])  4.33 us
    ppermute x1, starting transfers between devices, per_device(): left_main = lax.ppermute(main, 'blk', to_right)  3.93 us
    ppermute x1, starting transfers between devices, per_device(): right = lax.ppermute(own, 'blk', to_left)  3.4 us
    ppermute x1, waiting for transfers between devices, per_device(): other = lax.ppermute(sums, 'tp', [(i, i ^ 1) for i in range(peers)])  3.37 us
    pallas_call x1, Pallas kernels, per_device(): kernel_call(own_product, (jax.ShapeDtypeStruct((rank, rows + columns), f3...  2.42 us
  transfers between devices with their start and end apart: 6, of which 4 were waited for; matrix products, arithmetic and copies ran while one was open for 0% of the time, Pallas kernels for 3%

profile of v3, /device:TPU:2, one launch (start us, length us, event | category | flops | bytes accessed | tf_op | source)
XLA Modules:
  0.0 68.9 jit_solution(12318025945840190088)
XLA Ops:
  0.6 2.4 %shard_map.41 = (f32[8,4224]{1,0:T(8,128)S(1)}, bf16[3,128,4096]{2,1,0:T(8,128)(2,1)S(1)}, f32[2816,128]{1,0:T(8,128)S(1)}, f32[1280,128]{1,0:T(8,128)S(1)}) custom-call(f32[1,8,128]{2,1,0:T(8,128)} %q_hbm.1, f32[1,4096,128]{2,1,0:T(8,128)} %matrix_hbm.1), custom_call_target="tpu_custom_call" | custom-call | flops 50331648 | bytes 4194304 | tf_op jit(solution)/shard_map/pallas_call | solution.py:260
  3.1 1.9 %collective-permute-start.1 = (f32[8,4224]{1,0:T(8,128)S(1)}, f32[8,4224]{1,0:T(8,128)S(1)}, u32[]{:S(2)}, u32[]{:S(2)}) collective-permute-start(f32[8,4224]{1,0:T(8,128)S(1)} %get-tuple-element.18), channel_id=1, source_target_pairs={{0,8},{8,16},{16,24},{24,32},{32,40},{40,48},{48,56},{56,64},{64,7... | collective-permute-start | bytes 405512 | tf_op jit(solution)/shard_map/ppermute | solution.py:269
  5.0 3.9 %collective-permute-start.3 = (f32[2816,128]{1,0:T(8,128)S(1)}, f32[2816,128]{1,0:T(8,128)S(1)}, u32[]{:S(2)}, u32[]{:S(2)}) collective-permute-start(f32[2816,128]{1,0:T(8,128)S(1)} %get-tuple-element.16.mine_ref.main_ref), channel_id=1, source_target_pairs={{0,8},{8,16},{16,24},{24,32},{32,40},{40,48},{48,56},{56,64},{64,7... | collective-permute-start | bytes 4325384 | tf_op jit(solution)/shard_map/ppermute | solution.py:270
  8.9 0.7 %collective-permute-start = (f32[1280,128]{1,0:T(8,128)S(1)}, f32[1280,128]{1,0:T(8,128)S(1)}, u32[]{:S(2)}, u32[]{:S(2)}) collective-permute-start(f32[1280,128]{1,0:T(8,128)S(1)} %get-tuple-element.17.mine_ref.late_ref), channel_id=1, source_target_pairs={{0,0},{8,8},{16,16},{24,24},{32,32},{40,40},{48,48},{56,56},{64,64... | collective-permute-start | bytes 1966088 | tf_op jit(solution)/shard_map/ppermute | solution.py:271
  9.6 6.9 %collective-permute-done.1.packed_ref = f32[8,4224]{1,0:T(8,128)S(1)} collective-permute-done((f32[8,4224]{1,0:T(8,128)S(1)}, f32[8,4224]{1,0:T(8,128)S(1)}, u32[]{:S(2)}, u32[]{:S(2)}) %collective-permute-start.1) | collective-permute-done | bytes 135200 | tf_op jit(solution)/shard_map/ppermute | solution.py:269
  16.6 0.5 shard_map.42
  17.1 12.3 %all_to_all.10.sums_ref = f32[4,8,4096]{2,1,0:T(8,128)S(1)} all-to-all(f32[4,8,4096]{2,1,0:T(8,128)S(1)} %shard_map.42), channel_id=1, replica_groups={{0,2,4,6},{1,3,5,7},{8,10,12,14},{9,11,13,15},{16,18,20,22},{17,19,21,2..., dimensions={0} | all-to-all | bytes 1048576 | tf_op jit(solution)/shard_map/all_to_all | solution.py:220
  29.4 0.0 collective-permute-done
  29.4 0.0 collective-permute-start.4
  29.5 4.3 %collective-permute-start.2 = (f32[8,4096]{1,0:T(8,128)S(1)}, f32[8,4096]{1,0:T(8,128)S(1)}, u32[]{:S(2)}, u32[]{:S(2)}) collective-permute-start(f32[8,4096]{1,0:T(8,128)S(1)} %shard_map.43.sum_ref), channel_id=1, source_target_pairs={{0,1},{1,0},{2,3},{3,2},{4,5},{5,4},{6,7},{7,6},{8,9},{9,8},{10,11... | collective-permute-start | bytes 393224 | tf_op jit(solution)/shard_map/ppermute | solution.py:275
  33.8 0.0 collective-permute-done.3.left_ref
  33.8 0.6 shard_map.44
  34.5 3.4 %collective-permute-done.2.other_ref = f32[8,4096]{1,0:T(8,128)S(1)} collective-permute-done((f32[8,4096]{1,0:T(8,128)S(1)}, f32[8,4096]{1,0:T(8,128)S(1)}, u32[]{:S(2)}, u32[]{:S(2)}) %collective-permute-start.2) | collective-permute-done | bytes 131104 | tf_op jit(solution)/shard_map/ppermute | solution.py:275
  37.9 0.7 %shard_map.45 = (f32[8,1280]{1,0:T(8,128)S(1)}, f32[8,128]{1,0:T(8,128)S(1)}, f32[8,128]{1,0:T(8,128)S(1)}, f32[7,8,128]{2,1,0:T(8,128)S(1)}) custom-call(f32[8,4096]{1,0:T(8,128)S(1)} %shard_map.43.sum_ref, f32[8,4096]{1,0:T(8,128)S(1)} %collective-permute-done.2.other_ref, bf16[3,2816,128]{2,1,0:T(8,128)(2,1)S(1)} %get-tuple-element.21.main_ref), custom_call_target="tpu_custom_call" | custom-call | flops 50331648 | bytes 4194304 | tf_op jit(solution)/shard_map/pallas_call | solution.py:280
  38.6 2.1 %collective-permute-done.4.left_ref = f32[1280,128]{1,0:T(8,128)S(1)} collective-permute-done((f32[1280,128]{1,0:T(8,128)S(1)}, f32[1280,128]{1,0:T(8,128)S(1)}, u32[]{:S(2)}, u32[]{:S(2)}) %collective-permute-start.4) | collective-permute-done | bytes 655392 | tf_op jit(solution)/shard_map/ppermute | solution.py:274
  40.7 1.0 %shard_map.46 = (bf16[3,1280,128]{2,1,0:T(8,128)(2,1)S(1)}, f32[8,8,4096]{2,1,0:T(8,128)S(1)}) custom-call(f32[8,1280]{1,0:T(8,128)S(1)} %get-tuple-element.22.value_ref, f32[8,128]{1,0:T(8,128)S(1)} %get-tuple-element.23.image_ref, f32[8,128]{1,0:T(8,128)S(1)} %get-tuple-element.24.scale_ref, f32[7,8,128]{2,1,0:T(8,128)S(1)} %get-tuple-element.25.ratios_ref, ...), custom_call_target="tpu_custom_call" | custom-call | flops 50331648 | bytes 4194304 | tf_op jit(solution)/shard_map/pallas_call | solution.py:288
  41.7 18.6 %all_to_all.11.sums_ref = f32[8,8,4096]{2,1,0:T(8,128)S(1)} all-to-all(f32[8,8,4096]{2,1,0:T(8,128)S(1)} %get-tuple-element.28), channel_id=1, replica_groups=mesh['blk'=64,'tp'=8] {'tp'}, dimensions={0} | all-to-all | bytes 2097152 | tf_op jit(solution)/shard_map/all_to_all | solution.py:291
  60.3 0.9 %shard_map.47.packed_ref = f32[8,4352]{1,0:T(8,128)S(1)} custom-call(f32[8,8,4096]{2,1,0:T(8,128)S(1)} %all_to_all.11.sums_ref, bf16[3,2816,128]{2,1,0:T(8,128)(2,1)S(1)} %get-tuple-element.21.main_ref, bf16[3,1280,128]{2,1,0:T(8,128)(2,1)S(1)} %get-tuple-element.29.late_ref), custom_call_target="tpu_custom_call" | custom-call | flops 50331648 | bytes 4194304 | tf_op jit(solution)/shard_map/pallas_call | solution.py:292
  61.2 3.4 %collective-permute-start.5 = (f32[8,4352]{1,0:T(8,128)S(1)}, f32[8,4352]{1,0:T(8,128)S(1)}, u32[]{:S(2)}, u32[]{:S(2)}) collective-permute-start(f32[8,4352]{1,0:T(8,128)S(1)} %shard_map.47.packed_ref), channel_id=1, source_target_pairs={{0,504},{8,0},{16,8},{24,16},{32,24},{40,32},{48,40},{56,48},{64,5... | collective-permute-start | bytes 417800 | tf_op jit(solution)/shard_map/ppermute | solution.py:295
  64.6 0.5 shard_map.48.matrix_ref
  65.1 2.1 %collective-permute-done.5.packed_ref = f32[8,4352]{1,0:T(8,128)S(1)} collective-permute-done((f32[8,4352]{1,0:T(8,128)S(1)}, f32[8,4352]{1,0:T(8,128)S(1)}, u32[]{:S(2)}, u32[]{:S(2)}) %collective-permute-start.5) | collective-permute-done | bytes 139296 | tf_op jit(solution)/shard_map/ppermute | solution.py:295
  67.2 1.7 %shard_map.49 = (f32[1,4096,128]{2,1,0:T(8,128)}, f32[1,8,128]{2,1,0:T(8,128)}) custom-call(f32[4096,128]{1,0:T(8,128)S(1)} %shard_map.48.matrix_ref, f32[8,4352]{1,0:T(8,128)S(1)} %collective-permute-done.5.packed_ref), custom_call_target="tpu_custom_call" | custom-call | flops 50331648 | bytes 4194304 | tf_op jit(solution)/shard_map/pallas_call | solution.py:297
  (1 shorter events, 0.0 us)
Async XLA Ops:
  3.1 13.5 %collective-permute-start.1 = (f32[8,4224]{1,0:T(8,128)S(1)}, f32[8,4224]{1,0:T(8,128)S(1)}, u32[]{:S(2)}, u32[]{:S(2)}) collective-permute-start(f32[8,4224]{1,0:T(8,128)S(1)} %get-tuple-element.18), channel_id=1, source_target_pairs={{0,8},{8,16},{16,24},{24,32},{32,40},{40,48},{48,56},{56,64},{64,7... | collective-permute-start | bytes 405512 | tf_op jit(solution)/shard_map/ppermute | solution.py:269
  5.0 28.8 %collective-permute-start.3 = (f32[2816,128]{1,0:T(8,128)S(1)}, f32[2816,128]{1,0:T(8,128)S(1)}, u32[]{:S(2)}, u32[]{:S(2)}) collective-permute-start(f32[2816,128]{1,0:T(8,128)S(1)} %get-tuple-element.16.mine_ref.main_ref), channel_id=1, source_target_pairs={{0,8},{8,16},{16,24},{24,32},{32,40},{40,48},{48,56},{56,64},{64,7... | collective-permute-start | bytes 4325384 | tf_op jit(solution)/shard_map/ppermute | solution.py:270
  8.9 20.5 %collective-permute-start = (f32[1280,128]{1,0:T(8,128)S(1)}, f32[1280,128]{1,0:T(8,128)S(1)}, u32[]{:S(2)}, u32[]{:S(2)}) collective-permute-start(f32[1280,128]{1,0:T(8,128)S(1)} %get-tuple-element.17.mine_ref.late_ref), channel_id=1, source_target_pairs={{0,0},{8,8},{16,16},{24,24},{32,32},{40,40},{48,48},{56,56},{64,64... | collective-permute-start | bytes 1966088 | tf_op jit(solution)/shard_map/ppermute | solution.py:271
  29.4 11.2 %collective-permute-start.4 = (f32[1280,128]{1,0:T(8,128)S(1)}, f32[1280,128]{1,0:T(8,128)S(1)}, u32[]{:S(2)}, u32[]{:S(2)}) collective-permute-start(f32[1280,128]{1,0:T(8,128)S(1)} %collective-permute-done), channel_id=1, source_target_pairs={{0,8},{8,16},{16,24},{24,32},{32,40},{40,48},{48,56},{56,64},{64,7... | collective-permute-start | bytes 1966088 | tf_op jit(solution)/shard_map/ppermute | solution.py:274
  29.5 8.4 %collective-permute-start.2 = (f32[8,4096]{1,0:T(8,128)S(1)}, f32[8,4096]{1,0:T(8,128)S(1)}, u32[]{:S(2)}, u32[]{:S(2)}) collective-permute-start(f32[8,4096]{1,0:T(8,128)S(1)} %shard_map.43.sum_ref), channel_id=1, source_target_pairs={{0,1},{1,0},{2,3},{3,2},{4,5},{5,4},{6,7},{7,6},{8,9},{9,8},{10,11... | collective-permute-start | bytes 393224 | tf_op jit(solution)/shard_map/ppermute | solution.py:275
  61.2 6.0 %collective-permute-start.5 = (f32[8,4352]{1,0:T(8,128)S(1)}, f32[8,4352]{1,0:T(8,128)S(1)}, u32[]{:S(2)}, u32[]{:S(2)}) collective-permute-start(f32[8,4352]{1,0:T(8,128)S(1)} %shard_map.47.packed_ref), channel_id=1, source_target_pairs={{0,504},{8,0},{16,8},{24,16},{32,24},{40,32},{48,40},{56,48},{64,5... | collective-permute-start | bytes 417800 | tf_op jit(solution)/shard_map/ppermute | solution.py:295
